TPU v7x, 32 devices: a whole 2x2x4 slice. The times are simulated.
32 devices in a mesh: rows: 8 (over y, x, core), section: 4 (over z).
Axes of the slice: x: 2, y: 2, z: 4, core: 2. Of those that a mesh axis runs over, the one named last changes fastest.
Arguments:
- start_vec: float32 [16384, 2, 256], P('rows'), may hold values from -6 to 6
- left_vec: float32 [16384, 2, 256], P('rows'), may hold values from -6 to 6
- hamil: bfloat16 [128, 16, 2, 128, 128], P('rows', 'section'), may hold values from -0.109375 to 0.109375
- cols: int32 [128, 16], P('rows', 'section'), may hold values from 0 to 127, as said below
- live: int32 [128, 4], P('rows', 'section'), may hold values from 1 to 4, as said below
Outputs:
- moments: float32 [5, 256], replicated
- last_vec: float32 [16384, 2, 256], P('rows')
- before_vec: float32 [16384, 2, 256], P('rows')
Inputs may be any that keep to these rules, and one draw needn't show every extreme that they name: `cols`: each block column lies within 16 of its block row; slot 0 of every block row is the block row itself; a column may repeat in a row, and then its blocks add. `live`: loads differ between row groups.
All inputs are finite; a program needn't handle non-finite values.
Results may differ from a plain program's by a relative error of at most 0.0028.
Values may be sent and summed in bfloat16 or wider, within the bound.
A program may use at most 128 MiB of HBM per device.

v0:
```python
import jax
import jax.numpy as jnp
from jax import lax
from jax.sharding import PartitionSpec as P

REACH = 16
STEPS = 4


def padded(cells, sides, width):
    for axis, dim in sides:
        count = lax.axis_size(axis)
        ends = count - 1
        head = lax.slice_in_dim(cells, 0, width, axis=dim)
        tail = lax.slice_in_dim(cells, cells.shape[dim] - width, cells.shape[dim], axis=dim)
        cells = jnp.concatenate(
            [
                lax.ppermute(tail, axis, [(i, (i + 1) % count) for i in range(ends)]),
                cells,
                lax.ppermute(head, axis, [((i + 1) % count, i) for i in range(ends)]),
            ],
            axis=dim,
        )
    return cells


def complex_parts(out):
    real_part = out[:, 0, :, 0] - out[:, 1, :, 1]
    imag_part = out[:, 0, :, 1] + out[:, 1, :, 0]
    return jnp.stack([real_part, imag_part], axis=2)


def body(start_vec, left_vec, hamil, cols, live):
    row_blocks, slot_count = cols.shape
    block_size = hamil.shape[-1]
    base = lax.axis_index("rows") * row_blocks
    panel_index = cols - base + REACH
    mask_bf = (jnp.arange(slot_count)[None, :] < live).astype(jnp.bfloat16)
    scale = 1.0 / (2.0 * block_size * row_blocks) ** 0.5
    current = start_vec
    previous = start_vec
    table = [jnp.sum(left_vec * current, axis=(0, 1))]
    for step in range(STEPS):
        extended = padded(current.astype(jnp.bfloat16), (("rows", 0),), REACH * block_size)
        all_cols = extended.shape[2]
        blocks = extended.reshape(-1, block_size, 2, all_cols)
        panels = jnp.take(blocks, panel_index, axis=0) * mask_bf[:, :, None, None, None]
        out = jnp.einsum("bkqij,bkjpc->bqipc", hamil, panels, preferred_element_type=jnp.float32)
        summed = lax.psum(
            complex_parts(out).reshape(row_blocks * block_size, 2, all_cols), "section"
        )
        fresh = summed if step == 0 else 2.0 * summed - previous
        previous, current = (current, fresh)
        table.append(jnp.sum(left_vec * current, axis=(0, 1)))
    partial_value = jnp.stack(table, axis=0)
    moments = lax.psum(partial_value, "rows") * scale
    return (moments, current, previous)


def solution(mesh):
    return jax.shard_map(
        body,
        mesh=mesh,
        in_specs=(
            P("rows", None, None),
            P("rows", None, None),
            P("rows", "section", None, None, None),
            P("rows", "section"),
            P("rows", "section"),
        ),
        out_specs=(P(), P("rows", None, None), P("rows", None, None)),
        check_vma=False,
    )
```

profile of v0, /device:TPU:0, one launch (start us, length us, event | category | flops | bytes accessed | tf_op | source)
XLA Modules:
  0.0 1040.7 jit_solution(10793872942615279801)
XLA Ops:
  7.2 0.0 all-reduce.5.cloned.1.call-start
  7.2 2.4 copy.168
  9.6 3.7 collective-permute-start
  13.3 1.3 collective-permute-start.1
  14.6 0.1 copy.78
  14.7 0.1 reshape.262
  14.8 0.1 copy.76
  14.9 0.1 fusion.28
  15.0 0.9 collective-permute-done
  15.9 4.4 collective-permute-done.1
  20.3 3.4 pad_maximum_fusion
  23.7 3.1 copy.79
  26.8 8.3 gather_fusion
  35.1 10.4 %fusion.12 = f32[16,2,128,2,256]{4,2,1,3,0:T(8,128)} fusion(bf16[16,4,128,2,256]{4,2,3,1,0:T(8,128)(2,1)} %bitcast.79, pred[16,4]{1,0:T(8,128)(4,1)S(1)} %copy.76, bf16[16,4]{1,0:T(8,128)(2,1)S(1)} %fusion.28, bf16[16,4,2,128,128]{4,3,2,1,0:T(8,128)(2,1)} %param.9), kind=kOutput, calls=%fused_computation.37 | convolution fusion | flops 2155872256 | bytes 20971712 | tf_op jit(solution)/shard_map/bkqij,bkjpc->bqipc/dot_general | solution.py:48
  45.5 4.1 slice_subtract_fusion.3
  49.6 2.3 pad_maximum_fusion.4
  51.9 0.0 all-reduce.7.cloned.1.call-start
  52.0 196.5 %all-reduce.5.cloned.1.call-done = f32[2048,2,256]{2,0,1:T(8,128)} async-done(((f32[2048,2,256]{2,0,1:T(8,128)}), f32[2048,2,256]{2,0,1:T(8,128)}) %all-reduce.5.cloned.1.call-update) | async-done | bytes 4194320 | tf_op jit(solution)/shard_map/psum | solution.py:49
  248.5 2.4 convert_element_type.21
  250.9 1.9 collective-permute-start.2
  252.8 1.5 collective-permute-start.3
  254.3 2.2 collective-permute-done.2
  256.4 3.6 collective-permute-done.3
  260.0 13.9 %pad_maximum_fusion.1 = bf16[6144,2,256]{2,0,1:T(8,128)(2,1)S(1)} fusion(bf16[2048,2,256]{2,0,1:T(8,128)(2,1)S(1)} %collective-permute-done.3, bf16[2048,2,256]{2,0,1:T(8,128)(2,1)S(1)} %convert_element_type.21, bf16[2048,2,256]{2,0,1:T(8,128)(2,1)S(1)} %collective-permute-done.2), kind=kLoop, calls=%fused_computation.21 | loop fusion | flops 18874368 | bytes 12582912 | tf_op jit(solution)/shard_map/concatenate | solution.py:16
  273.9 3.1 copy.85
  277.0 8.3 gather_fusion.1
  285.3 10.4 %fusion.15 = f32[16,2,128,2,256]{4,2,1,3,0:T(8,128)} fusion(bf16[16,4,128,2,256]{4,2,3,1,0:T(8,128)(2,1)} %bitcast.80, pred[16,4]{1,0:T(8,128)(4,1)S(1)} %copy.76, bf16[16,4]{1,0:T(8,128)(2,1)S(1)} %fusion.28, bf16[16,4,2,128,128]{4,3,2,1,0:T(8,128)(2,1)} %param.9), kind=kOutput, calls=%fused_computation.38 | convolution fusion | flops 2155872256 | bytes 20971712 | tf_op jit(solution)/shard_map/bkqij,bkjpc->bqipc/dot_general | solution.py:48
  295.8 4.1 slice_subtract_fusion.2
  299.9 2.3 pad_maximum_fusion.5
  302.1 0.0 all-reduce.7.cloned.1.call-update
  302.2 0.0 all-reduce.9.cloned.1.call-start
  302.2 194.3 %all-reduce.7.cloned.1.call-done = f32[2048,2,256]{2,0,1:T(8,128)} async-done(((f32[2048,2,256]{2,0,1:T(8,128)}), f32[2048,2,256]{2,0,1:T(8,128)}) %all-reduce.7.cloned.1.call-update) | async-done | bytes 4194320 | tf_op jit(solution)/shard_map/psum | solution.py:49
  496.5 4.1 fusion.29
  500.6 1.9 collective-permute-start.4
  502.5 1.5 collective-permute-start.5
  504.0 2.1 collective-permute-done.4
  506.1 3.6 collective-permute-done.5
  509.7 14.0 %pad_maximum_fusion.2 = bf16[6144,2,256]{2,0,1:T(8,128)(2,1)S(1)} fusion(bf16[2048,2,256]{2,0,1:T(8,128)(2,1)S(1)} %collective-permute-done.5, bf16[2048,2,256]{2,0,1:T(8,128)(2,1)S(1)} %fusion.29, bf16[2048,2,256]{2,0,1:T(8,128)(2,1)S(1)} %collective-permute-done.4), kind=kLoop, calls=%fused_computation.22 | loop fusion | flops 18874368 | bytes 12582912 | tf_op jit(solution)/shard_map/concatenate | solution.py:16
  523.7 3.1 copy.92
  526.8 8.3 gather_fusion.2
  535.1 10.4 %fusion.18 = f32[16,2,128,2,256]{4,2,1,3,0:T(8,128)} fusion(bf16[16,4,128,2,256]{4,2,3,1,0:T(8,128)(2,1)} %bitcast.81, pred[16,4]{1,0:T(8,128)(4,1)S(1)} %copy.76, bf16[16,4]{1,0:T(8,128)(2,1)S(1)} %fusion.28, bf16[16,4,2,128,128]{4,3,2,1,0:T(8,128)(2,1)} %param.9), kind=kOutput, calls=%fused_computation.39 | convolution fusion | flops 2155872256 | bytes 20971712 | tf_op jit(solution)/shard_map/bkqij,bkjpc->bqipc/dot_general | solution.py:48
  545.5 4.1 slice_subtract_fusion.1
  549.6 2.3 pad_maximum_fusion.6
  551.9 0.0 all-reduce.9.cloned.1.call-update
  551.9 0.0 all-reduce.11.cloned.1.call-start
  552.0 194.3 %all-reduce.9.cloned.1.call-done = f32[2048,2,256]{2,0,1:T(8,128)} async-done(((f32[2048,2,256]{2,0,1:T(8,128)}), f32[2048,2,256]{2,0,1:T(8,128)}) %all-reduce.9.cloned.1.call-update) | async-done | bytes 4194320 | tf_op jit(solution)/shard_map/psum | solution.py:49
  746.3 6.1 fusion.30
  752.4 1.9 collective-permute-start.6
  754.3 1.7 collective-permute-start.7
  756.0 1.9 collective-permute-done.6
  757.9 3.6 collective-permute-done.7
  761.5 13.8 %pad_maximum_fusion.3 = bf16[6144,2,256]{2,0,1:T(8,128)(2,1)S(1)} fusion(bf16[2048,2,256]{2,0,1:T(8,128)(2,1)S(1)} %collective-permute-done.7, bf16[2048,2,256]{2,0,1:T(8,128)(2,1)S(1)} %get-tuple-element.12, bf16[2048,2,256]{2,0,1:T(8,128)(2,1)S(1)} %collective-permute-done.6), kind=kLoop, calls=%fused_computation.23 | loop fusion | flops 18874368 | bytes 12582912 | tf_op jit(solution)/shard_map/concatenate | solution.py:16
  775.3 3.1 copy.98
  778.4 8.3 gather_fusion.3
  786.7 10.4 %fusion.21 = f32[16,2,128,2,256]{4,2,1,3,0:T(8,128)} fusion(bf16[16,4,128,2,256]{4,2,3,1,0:T(8,128)(2,1)} %bitcast.78, pred[16,4]{1,0:T(8,128)(4,1)S(1)} %copy.76, bf16[16,4]{1,0:T(8,128)(2,1)S(1)} %fusion.28, bf16[16,4,2,128,128]{4,3,2,1,0:T(8,128)(2,1)} %param.9), kind=kOutput, calls=%fused_computation.40 | convolution fusion | flops 2155872256 | bytes 20971712 | tf_op jit(solution)/shard_map/bkqij,bkjpc->bqipc/dot_general | solution.py:48
  797.2 4.1 slice_subtract_fusion
  801.3 2.2 pad_maximum_fusion.7
  803.5 6.6 multiply_reduce_fusion.4
  810.2 12.4 %copy.103 = f32[2048,2,256]{2,1,0:T(2,128)} copy(f32[2048,2,256]{2,0,1:T(8,128)S(1)} %copy-done) | data formatting | bytes 8388608
  822.5 175.4 %all-reduce.11.cloned.1.call-done = f32[2048,2,256]{2,0,1:T(8,128)} async-done(((f32[2048,2,256]{2,0,1:T(8,128)}), f32[2048,2,256]{2,0,1:T(8,128)}) %all-reduce.11.cloned.1.call-update) | async-done | bytes 4194320 | tf_op jit(solution)/shard_map/psum | solution.py:49
  997.9 9.4 multiply_reduce_fusion
  1007.3 12.2 %copy.102 = f32[2048,2,256]{2,1,0:T(2,128)} copy(f32[2048,2,256]{2,0,1:T(8,128)S(1)} %get-tuple-element.11) | data formatting | bytes 8388608
  1019.5 13.9 %psum.39 = f32[5,256]{1,0:T(8,128)S(1)} all-reduce(f32[5,256]{1,0:T(8,128)S(1)} %stack.47), channel_id=1, replica_groups=mesh['rows'=8,'section'=4] {'rows'}, use_global_device_ids=true, to_apply=%region_9.11 | all-reduce | flops 1280 | bytes 10240 | tf_op jit(solution)/shard_map/psum | solution.py:56
  1033.4 0.6 broadcast_multiply_fusion
  (11 shorter events, 0.1 us)
Async XLA Ops:
  7.2 7.5 copy-start.1
  7.2 7.7 copy-start.2
  7.2 241.3 %all-reduce.5.cloned.1.call-start = ((), (), s32[]{:S(2)}) async-start(), calls=%async_computation | async-start | bytes 8388608 | tf_op jit(solution)/shard_map/psum | solution.py:49
  9.6 6.3 collective-permute-start
  13.3 7.0 collective-permute-start.1
  51.9 444.6 %all-reduce.7.cloned.1.call-start = ((), (), s32[]{:S(2)}) async-start(), calls=%async_computation.1 | async-start | bytes 8388608 | tf_op jit(solution)/shard_map/psum | solution.py:49
  250.9 5.5 collective-permute-start.2
  252.8 7.2 collective-permute-start.3
  302.2 444.1 %all-reduce.9.cloned.1.call-start = ((), (), s32[]{:S(2)}) async-start(), calls=%async_computation.2 | async-start | bytes 8388608 | tf_op jit(solution)/shard_map/psum | solution.py:49
  500.6 5.5 collective-permute-start.4
  502.5 7.2 collective-permute-start.5
  551.9 446.0 %all-reduce.11.cloned.1.call-start = ((), (), s32[]{:S(2)}) async-start(), calls=%async_computation.3 | async-start | bytes 8388608 | tf_op jit(solution)/shard_map/psum | solution.py:49
  752.4 5.5 collective-permute-start.6
  754.3 7.2 collective-permute-start.7
  803.5 6.6 copy-start
Sparse Core Ops, SparseCore 0:
  52.1 196.4 all-reduce.4
  302.3 194.2 all-reduce.6
  552.1 194.1 all-reduce.8
  803.6 194.2 all-reduce.10
where the time goes:
time: 1050 us; the launch traced here: 1040 us
  waiting for transfers between devices  783 us (75%)
  other arithmetic  99.7 us (9%)
  local copies, waits for them, and re-layouts  73 us (7%)
  matrix products  41.7 us (4%)
  starting transfers between devices  15.4 us (1%)
  between operations  14.2 us (1%)
  blocking collectives  13.9 us (1%)
    psum x4, waiting for transfers between devices, body(): lax.psum(complex_parts(out).reshape(row_blocks * block_size, 2, all_cols)...  761 us
    concatenate x4, other arithmetic, padded(): jnp.concatenate([lax.ppermute(tail, axis, [(i, (i + 1) % count) for i in...  45 us
    dot_general x4, matrix products, body(): jnp.einsum('bkqij,bkjpc->bqipc', hamil, panels, preferred_element_type=jn...  41.7 us
    gather x4, local copies, waits for them, and re-layouts, body(): jnp.take(blocks, panel_index, axis=0) * mask_bf[:, :, None, None, None]  33.2 us
    unnamed x9, local copies, waits for them, and re-layouts  27 us
  transfers between devices with their start and end apart: 12, of which 12 were waited for; matrix products, arithmetic and copies ran while one was open for 2% of the time, Pallas kernels for 0%

commit v1 on v0

--- a/solution.py
+++ b/solution.py
@@ -46,8 +46,11 @@
         blocks = extended.reshape(-1, block_size, 2, all_cols)
         panels = jnp.take(blocks, panel_index, axis=0) * mask_bf[:, :, None, None, None]
         out = jnp.einsum("bkqij,bkjpc->bqipc", hamil, panels, preferred_element_type=jnp.float32)
-        summed = lax.psum(
-            complex_parts(out).reshape(row_blocks * block_size, 2, all_cols), "section"
+        summed = jnp.sum(
+            lax.all_gather(
+                complex_parts(out).reshape(row_blocks * block_size, 2, all_cols), "section"
+            ),
+            axis=0,
         )
         fresh = summed if step == 0 else 2.0 * summed - previous
         previous, current = (current, fresh)

time: 1050 us -> 1610 us (1.53)
  waiting for transfers between devices: 783 us -> 1310 us
  other arithmetic: 99.7 us -> 137 us
    all_gather x0 -> x4, waiting for transfers between devices: none -> 1280 us  [body(): lax.all_gather(complex_parts(out).reshape(row_blocks * block_size, 2, all...]
    psum x4 -> x0, waiting for transfers between devices: 761 us -> none  [body(): lax.psum(complex_parts(out).reshape(row_blocks * block_size, 2, all_cols)...]
    reduce_sum x0 -> x4, other arithmetic: none -> 37.8 us  [body(): jnp.sum(lax.all_gather(complex_parts(out).reshape(row_blocks * block_size...]
  transfers between devices with their start and end apart: 12 -> 12, of which waited for: 12 -> 12; matrix products, arithmetic and copies ran while one was open for 2% -> 1% of each run, Pallas kernels for 0% -> 0%
where the time goes in v1:
time: 1610 us; the launch traced here: 1600 us
  waiting for transfers between devices  1310 us (81%)
  other arithmetic  137 us (9%)
  local copies, waits for them, and re-layouts  73 us (5%)
  matrix products  41.7 us (3%)
    all_gather x4, waiting for transfers between devices, body(): lax.all_gather(complex_parts(out).reshape(row_blocks * block_size, 2, all...  1280 us
    concatenate x4, other arithmetic, padded(): jnp.concatenate([lax.ppermute(tail, axis, [(i, (i + 1) % count) for i in...  45 us
    dot_general x4, matrix products, body(): jnp.einsum('bkqij,bkjpc->bqipc', hamil, panels, preferred_element_type=jn...  41.7 us
    reduce_sum x4, other arithmetic, body(): jnp.sum(lax.all_gather(complex_parts(out).reshape(row_blocks * block_size...  37.8 us
    gather x4, local copies, waits for them, and re-layouts, body(): jnp.take(blocks, panel_index, axis=0) * mask_bf[:, :, None, None, None]  33.2 us
  transfers between devices with their start and end apart: 12, of which 12 were waited for; matrix products, arithmetic and copies ran while one was open for 1% of the time, Pallas kernels for 0%

profile of v1, /device:TPU:0, one launch (start us, length us, event | category | flops | bytes accessed | tf_op | source)
XLA Modules:
  0.0 1603.4 jit_solution(3834370951352924915)
XLA Ops:
  7.2 2.4 copy.172
  9.6 3.7 collective-permute-start
  13.3 1.3 collective-permute-start.1
  14.6 0.1 copy.82
  14.7 0.1 reshape.258
  14.8 0.1 copy.80
  14.9 0.1 fusion.28
  15.0 0.9 collective-permute-done
  15.9 4.4 collective-permute-done.1
  20.3 3.4 pad_maximum_fusion
  23.7 3.1 copy.83
  26.8 8.3 gather_fusion
  35.1 10.4 fusion.12
  45.5 4.1 slice_subtract_fusion.3
  49.6 2.3 pad_maximum_fusion.4
  52.0 328.3 %all-gather.5.cloned.1.call-done = f32[4,2048,2,256]{3,1,2,0:T(8,128)} async-done(((f32[1,2048,2,256]{3,1,2,0:T(8,128)}), f32[4,2048,2,256]{3,1,2,0:T(8,128)}) %all-gather.5.cloned.1.call-update) | async-done | bytes 16777232 | tf_op jit(solution)/shard_map/all_gather | solution.py:50
  380.3 9.5 reduce_sum.82
  389.8 2.4 convert_element_type.21
  392.2 2.1 collective-permute-start.2
  394.3 1.5 collective-permute-start.3
  395.8 2.2 collective-permute-done.2
  397.9 3.3 collective-permute-done.3
  401.2 13.9 pad_maximum_fusion.1
  415.1 3.1 copy.89
  418.3 8.3 gather_fusion.1
  426.6 10.4 fusion.15
  437.0 4.1 slice_subtract_fusion.2
  441.1 2.3 pad_maximum_fusion.5
  443.4 0.4 all-gather.9.cloned.1.call-start
  443.9 324.9 %all-gather.7.cloned.1.call-done = f32[4,2048,2,256]{3,1,2,0:T(8,128)} async-done(((f32[1,2048,2,256]{3,1,2,0:T(8,128)}), f32[4,2048,2,256]{3,1,2,0:T(8,128)}) %all-gather.7.cloned.1.call-update) | async-done | bytes 16777232 | tf_op jit(solution)/shard_map/all_gather | solution.py:50
  768.8 9.4 reduce_sum.84
  778.2 4.1 fusion.29
  782.3 2.1 collective-permute-start.4
  784.4 1.3 collective-permute-start.5
  785.7 2.3 collective-permute-done.4
  788.0 3.3 collective-permute-done.5
  791.3 14.0 pad_maximum_fusion.2
  805.3 3.1 copy.96
  808.4 8.3 gather_fusion.2
  816.7 10.4 fusion.18
  827.1 4.1 slice_subtract_fusion.1
  831.2 2.3 pad_maximum_fusion.6
  833.5 0.2 all-gather.11.cloned.1.call-start
  833.8 325.2 %all-gather.9.cloned.1.call-done = f32[4,2048,2,256]{3,1,2,0:T(8,128)} async-done(((f32[1,2048,2,256]{3,1,2,0:T(8,128)}), f32[4,2048,2,256]{3,1,2,0:T(8,128)}) %all-gather.9.cloned.1.call-update) | async-done | bytes 16777232 | tf_op jit(solution)/shard_map/all_gather | solution.py:50
  1158.9 9.5 reduce_sum.86
  1168.4 6.0 fusion.30
  1174.4 2.1 collective-permute-start.6
  1176.5 1.3 collective-permute-start.7
  1177.8 2.3 collective-permute-done.6
  1180.2 3.3 collective-permute-done.7
  1183.5 13.8 pad_maximum_fusion.3
  1197.3 3.1 copy.102
  1200.4 8.3 gather_fusion.3
  1208.7 10.4 fusion.21
  1219.1 4.1 slice_subtract_fusion
  1223.2 2.2 pad_maximum_fusion.7
  1225.5 6.6 multiply_reduce_fusion.4
  1232.1 12.4 copy.107
  1244.6 306.3 %all-gather.11.cloned.1.call-done = f32[4,2048,2,256]{3,1,2,0:T(8,128)} async-done(((f32[1,2048,2,256]{3,1,2,0:T(8,128)}), f32[4,2048,2,256]{3,1,2,0:T(8,128)}) %all-gather.11.cloned.1.call-update) | async-done | bytes 16777232 | tf_op jit(solution)/shard_map/all_gather | solution.py:50
  1550.9 9.4 reduce_sum.88
  1560.3 9.4 multiply_reduce_fusion
  1569.7 12.2 copy.106
  1581.9 14.1 psum.7
  1596.0 0.6 broadcast_multiply_fusion
  (15 shorter events, 0.2 us)
Async XLA Ops:
  7.2 7.5 copy-start.1
  7.2 7.7 copy-start.2
  7.2 373.1 %all-gather.5.cloned.1.call-start = ((), (), s32[]{:S(2)}) async-start(), calls=%async_computation | async-start | bytes 20971520 | tf_op jit(solution)/shard_map/all_gather | solution.py:50
  9.6 6.3 collective-permute-start
  13.3 7.0 collective-permute-start.1
  51.9 716.9 %all-gather.7.cloned.1.call-start = ((), (), s32[]{:S(2)}) async-start(), calls=%async_computation.1 | async-start | bytes 20971520 | tf_op jit(solution)/shard_map/all_gather | solution.py:50
  392.2 5.7 collective-permute-start.2
  394.3 7.0 collective-permute-start.3
  443.4 715.5 %all-gather.9.cloned.1.call-start = ((), (), s32[]{:S(2)}) async-start(), calls=%async_computation.2 | async-start | bytes 20971520 | tf_op jit(solution)/shard_map/all_gather | solution.py:50
  782.3 5.7 collective-permute-start.4
  784.4 7.0 collective-permute-start.5
  833.5 717.4 %all-gather.11.cloned.1.call-start = ((), (), s32[]{:S(2)}) async-start(), calls=%async_computation.3 | async-start | bytes 20971520 | tf_op jit(solution)/shard_map/all_gather | solution.py:50
  1174.4 5.7 collective-permute-start.6
  1176.5 7.0 collective-permute-start.7
  1225.5 6.6 copy-start
Sparse Core Ops, SparseCore 0:
  52.1 328.2 all-gather.4
  443.5 325.2 all-gather.6
  833.7 325.2 all-gather.8
  1225.6 325.2 all-gather.10
